TPU v7x, 32 devices: a whole 2x2x4 slice. The times are simulated.
32 devices in a mesh: shot: 16 (over z, y, core), surf: 2 (over x).
Axes of the slice: x: 2, y: 2, z: 4, core: 2. Of those that a mesh axis runs over, the one named last changes fastest.
Arguments:
- down_data: bfloat16 [128, 16, 1024], P('shot', 'surf'), may hold values from -1.5 to 1.5
- up_data: bfloat16 [16, 512, 1024], P('surf', 'shot'), may hold values from -6 to 6
- taper_len: int32 [512], P('surf'), may hold values from 0 to 511
Outputs:
- multiples: bfloat16 [512, 128, 1024], P('surf', 'shot')
All inputs are finite; a program needn't handle non-finite values.
Results may differ from a plain program's by a relative error of at most 0.0082.
Values may be sent and summed in bfloat16 or wider, within the bound.
A program may use at most 128 MiB of HBM per device.

v0:
```python
import math

import jax
import jax.numpy as jnp
from jax import lax
from jax.sharding import PartitionSpec as P


def make_tables(samples):
    freqs = samples // 2
    times = jnp.arange(samples, dtype=jnp.int32)
    levels = jnp.arange(freqs, dtype=jnp.int32)
    phase = (levels[:, None] * times[None, :] % samples).astype(jnp.float32) * jnp.float32(
        2.0 * math.pi / samples
    )
    cosine = jnp.cos(phase)
    sine = jnp.sin(phase)
    norm_factor = jnp.float32(1.0 / math.sqrt(samples))
    forward_table = (jnp.concatenate([cosine.T, -sine.T], axis=1) * norm_factor).astype(
        jnp.bfloat16
    )
    weights = jnp.where(levels == 0, jnp.float32(1.0), jnp.float32(2.0))[:, None]
    inverse_table = (
        jnp.concatenate([weights * cosine, -weights * sine], axis=0) * norm_factor
    ).astype(jnp.bfloat16)
    return (forward_table, inverse_table)


def body(down_data, up_data, taper_len):
    samples = down_data.shape[2]
    freqs = samples // 2
    shots_here = down_data.shape[0]
    points_here = down_data.shape[1]
    forward_table, inverse_table = make_tables(samples)
    down_spec = jnp.dot(
        down_data.reshape(shots_here * points_here, samples),
        forward_table,
        preferred_element_type=jnp.float32,
    )
    down_spec = down_spec.astype(jnp.bfloat16).reshape(shots_here, points_here, 2 * freqs)
    down_real = down_spec[:, :, :freqs]
    down_imag = down_spec[:, :, freqs:]
    piece = lax.all_gather(up_data, "shot", axis=1, tiled=True)
    flat = jnp.dot(piece.reshape(-1, samples), forward_table, preferred_element_type=jnp.float32)
    up_spec = flat.astype(jnp.bfloat16).reshape(piece.shape[0], piece.shape[1], 2 * freqs)
    receivers = up_spec.shape[1]
    rows_out = receivers // lax.axis_size("surf")
    up_real = up_spec[:, :, :freqs]
    up_imag = up_spec[:, :, freqs:]
    real_part = jnp.einsum(
        "skf,krf->rsf", down_real, up_real, preferred_element_type=jnp.float32
    ) - jnp.einsum("skf,krf->rsf", down_imag, up_imag, preferred_element_type=jnp.float32)
    imag_part = jnp.einsum(
        "skf,krf->rsf", down_real, up_imag, preferred_element_type=jnp.float32
    ) + jnp.einsum("skf,krf->rsf", down_imag, up_real, preferred_element_type=jnp.float32)
    partial_g = jnp.concatenate([real_part, imag_part], axis=2).astype(jnp.bfloat16)
    total = lax.psum_scatter(
        partial_g.astype(jnp.float32).astype(jnp.bfloat16), "surf", scatter_dimension=0, tiled=True
    ).astype(jnp.float32)
    total = total.astype(jnp.bfloat16)
    trace = jnp.dot(
        total.reshape(rows_out * shots_here, 2 * freqs),
        inverse_table,
        preferred_element_type=jnp.float32,
    )
    trace = trace.reshape(rows_out, shots_here, samples)
    ramp_len = samples // 16
    sample_pos = jnp.arange(samples, dtype=jnp.float32)
    mute = jnp.clip(
        (sample_pos[None, :] - taper_len.astype(jnp.float32)[:, None] + ramp_len) / ramp_len,
        0.0,
        1.0,
    )
    return (trace * mute[:, None, :]).astype(jnp.bfloat16)


def solution(mesh):
    placed = (P("shot", "surf", None), P("surf", "shot", None), P("surf"))
    return jax.shard_map(
        body, mesh=mesh, in_specs=placed, out_specs=P("surf", "shot", None), check_vma=False
    )
```

profile of v0, /device:TPU:2, one launch (start us, length us, event | category | flops | bytes accessed | tf_op | source)
XLA Modules:
  0.0 332.5 jit_solution(5160586047615796318)
XLA Ops:
  6.5 0.0 copy-start
  6.5 0.0 all-gather.2.cloned.1.call-start
  6.5 0.7 all-gather.2.cloned.1.call-update
  7.3 0.0 reduce-scatter.2.cloned.1.call-start
  7.3 8.2 %sine_negate_fusion = (f32[1024,512]{1,0:T(8,128)S(1)}, f32[1024,512]{1,0:T(8,128)S(1)}) fusion(), kind=kLoop, calls=%fused_computation.29 | loop fusion | flops 7864320 | bytes 4194304 | tf_op jit(solution)/shard_map/neg | solution.py:19
  15.5 0.0 copy-start.3
  15.6 1.3 copy-done.3
  16.9 0.0 copy-done
  16.9 0.5 fusion.19
  17.4 1.7 copy.5
  19.1 0.7 copy.7
  19.8 66.0 %all-gather.2.cloned.1.call-done = bf16[8,512,1024]{2,1,0:T(8,128)(2,1)} async-done(((bf16[8,32,1024]{2,1,0:T(8,128)(2,1)}), bf16[8,512,1024]{2,1,0:T(8,128)(2,1)}) %all-gather.2.cloned.1.call-update) | async-done | bytes 8388624 | tf_op jit(solution)/shard_map/all_gather | solution.py:43
  85.8 25.2 %convolution_convert_fusion = bf16[1024,4096]{1,0:T(8,128)(2,1)} fusion(bf16[4096,1024]{1,0:T(8,128)(2,1)} %bitcast.35, f32[1024,512]{1,0:T(8,128)S(1)} %get-tuple-element.7, f32[1024,512]{1,0:T(8,128)} %copy-done.3), kind=kOutput, calls=%fused_computation.4 | convolution fusion | flops 8597274624 | bytes 20971520 | tf_op jit(solution)/shard_map/dot_general | solution.py:44
  111.1 12.2 %copy.11 = bf16[128,8,8,512]{3,2,1,0:T(8,128)(2,1)} copy(bf16[128,8,8,512]{3,1,2,0:T(8,128)(2,1)} %bitcast.34) | data formatting | bytes 16777216
  123.2 6.8 %fusion.34 = f32[512,512,8]{1,2,0:T(8,128)} fusion(bf16[8,512,1024]{1,0,2:T(8,128)(2,1)} %bitcast.30, bf16[8,8,512]{0,1,2:T(8,128)(2,1)S(1)} %copy.7), kind=kOutput, calls=%fused_computation.50 | convolution fusion | flops 33554432 | bytes 16842752 | tf_op jit(solution)/shard_map/skf,krf->rsf/dot_general | solution.py:52
  130.1 0.0 copy-start.2
  130.1 6.9 %fusion.36 = f32[512,512,8]{1,2,0:T(8,128)} fusion(bf16[8,512,1024]{1,0,2:T(8,128)(2,1)} %bitcast.31, bf16[8,8,512]{0,1,2:T(8,128)(2,1)S(1)} %copy.7), kind=kOutput, calls=%fused_computation.52 | convolution fusion | flops 33554432 | bytes 16842752 | tf_op jit(solution)/shard_map/skf,krf->rsf/dot_general | solution.py:55
  137.0 0.0 copy-done.2
  137.0 6.8 %fusion.33 = f32[512,512,8]{1,2,0:T(8,128)} fusion(bf16[8,512,1024]{1,0,2:T(8,128)(2,1)} %bitcast.32, bf16[8,8,512]{0,1,2:T(8,128)(2,1)S(1)} %copy-done.2), kind=kOutput, calls=%fused_computation.49 | convolution fusion | flops 33554432 | bytes 16842752 | tf_op jit(solution)/shard_map/skf,krf->rsf/dot_general | solution.py:50
  143.8 6.8 %fusion.35 = f32[512,512,8]{1,2,0:T(8,128)} fusion(bf16[8,512,1024]{1,0,2:T(8,128)(2,1)} %bitcast.33, bf16[8,8,512]{0,1,2:T(8,128)(2,1)S(1)} %copy-done.2), kind=kOutput, calls=%fused_computation.51 | convolution fusion | flops 33554432 | bytes 16842752 | tf_op jit(solution)/shard_map/skf,krf->rsf/dot_general | solution.py:53
  150.6 9.9 %copy.6 = f32[512,512,8]{0,1,2:T(8,128)} copy(f32[512,512,8]{1,2,0:T(8,128)} %fusion.33) | data formatting | bytes 16777216 | tf_op jit(solution)/shard_map/skf,krf->rsf/dot_general | solution.py:50
  160.6 9.9 %copy.8 = f32[512,512,8]{0,1,2:T(8,128)} copy(f32[512,512,8]{1,2,0:T(8,128)} %fusion.34) | data formatting | bytes 16777216 | tf_op jit(solution)/shard_map/skf,krf->rsf/dot_general | solution.py:52
  170.5 9.9 %copy.10 = f32[512,512,8]{0,1,2:T(8,128)} copy(f32[512,512,8]{1,2,0:T(8,128)} %fusion.36) | data formatting | bytes 16777216 | tf_op jit(solution)/shard_map/skf,krf->rsf/dot_general | solution.py:55
  180.4 10.0 %copy.9 = f32[512,512,8]{0,1,2:T(8,128)} copy(f32[512,512,8]{1,2,0:T(8,128)} %fusion.35) | data formatting | bytes 16777216 | tf_op jit(solution)/shard_map/skf,krf->rsf/dot_general | solution.py:53
  190.4 9.4 %fusion = bf16[512,8,512]{2,0,1:T(8,128)(2,1)} fusion(f32[512,512,8]{0,1,2:T(8,128)} %copy.6, f32[512,512,8]{0,1,2:T(8,128)} %copy.8), kind=kLoop, calls=%fused_computation.5 | loop fusion | flops 4194304 | bytes 20971520 | tf_op jit(solution)/shard_map/sub | solution.py:50
  199.9 9.3 %fusion.1 = bf16[512,8,512]{2,0,1:T(8,128)(2,1)} fusion(f32[512,512,8]{0,1,2:T(8,128)} %copy.9, f32[512,512,8]{0,1,2:T(8,128)} %copy.10), kind=kLoop, calls=%fused_computation.6 | loop fusion | flops 4194304 | bytes 20971520 | tf_op jit(solution)/shard_map/add | solution.py:53
  209.2 7.8 %pad_maximum_fusion = bf16[512,8,1024]{2,0,1:T(8,128)(2,1)} fusion(bf16[512,8,512]{2,0,1:T(8,128)(2,1)} %fusion.1, bf16[512,8,512]{2,0,1:T(8,128)(2,1)} %fusion), kind=kLoop, calls=%fused_computation | loop fusion | flops 16777216 | bytes 16777216 | tf_op jit(solution)/shard_map/concatenate | solution.py:56
  216.9 0.0 copy-start.4
  216.9 0.0 reduce-scatter.2.cloned.1.call-update
  217.0 0.7 copy-done.4
  217.6 0.2 multiply_clamp_fusion
  217.8 9.5 %sine_multiply_fusion = (f32[512,1024]{1,0:T(8,128)S(1)}, f32[512,1024]{1,0:T(8,128)}) fusion(f32[512]{0:T(512)S(1)} %fusion.25, f32[512]{0:T(512)S(1)} %fusion.24), kind=kLoop, calls=%fused_computation.24 | loop fusion | flops 8388608 | bytes 4198400 | tf_op jit(solution)/shard_map/mul | solution.py:24
  227.3 86.1 %reduce-scatter.2.cloned.1.call-done = bf16[256,8,1024]{2,0,1:T(8,128)(2,1)} async-done(((bf16[512,8,1024]{2,0,1:T(8,128)(2,1)}), bf16[256,8,1024]{2,0,1:T(8,128)(2,1)}) %reduce-scatter.2.cloned.1.call-update) | async-done | bytes 4194320 | tf_op jit(solution)/shard_map/reduce_scatter | solution.py:57
  313.5 0.0 copy-start.1
  313.5 7.4 %multiply_convert_fusion = bf16[256,8,1024]{2,0,1:T(8,128)(2,1)S(1)} fusion(f32[256,1024]{1,0:T(8,128)S(1)} %multiply_clamp_fusion, bf16[256,8,1024]{2,0,1:T(8,128)(2,1)} %reduce-scatter.2.cloned.1.call-done, f32[512,1024]{1,0:T(8,128)S(1)} %get-tuple-element.9, f32[512,1024]{1,0:T(8,128)} %get-tuple-element.10), kind=kOutput, calls=%fused_computation.1 | convolution fusion | flops 4302307328 | bytes 13631488 | tf_op jit(solution)/shard_map/dot_general | solution.py:61
  320.9 4.3 %copy.4 = bf16[256,8,1024]{2,1,0:T(8,128)(2,1)} copy(bf16[256,8,1024]{2,0,1:T(8,128)(2,1)S(1)} %multiply_convert_fusion) | data formatting | bytes 8388608 | tf_op jit(solution)/shard_map/convert_element_type | solution.py:74
  325.2 0.0 copy-done.1
  (4 shorter events, 0.0 us)
Async XLA Ops:
  6.5 10.3 %copy-start = (bf16[8,8,1024]{2,1,0:T(8,128)(2,1)S(1)}, bf16[8,8,1024]{2,1,0:T(8,128)(2,1)}, u32[]{:S(2)}) copy-start(bf16[8,8,1024]{2,1,0:T(8,128)(2,1)} %param.3) | copy-start | bytes 393220
  6.5 79.3 %all-gather.2.cloned.1.call-start = ((), (), s32[]{:S(2)}) async-start(), calls=%async_computation.1 | async-start | bytes 8912896 | tf_op jit(solution)/shard_map/all_gather | solution.py:43
  7.3 306.2 %reduce-scatter.2.cloned.1.call-start = ((), (), s32[]{:S(2)}) async-start(), calls=%async_computation.2 | async-start | bytes 12582912 | tf_op jit(solution)/shard_map/reduce_scatter | solution.py:57
  15.5 1.3 copy-start.3
  130.1 6.9 %copy-start.2 = (bf16[8,8,512]{0,1,2:T(8,128)(2,1)S(1)}, bf16[8,8,512]{0,1,2:T(8,128)(2,1)}, u32[]{:S(2)}) copy-start(bf16[8,8,512]{0,1,2:T(8,128)(2,1)} %copy.5) | copy-start | bytes 196612
  216.9 0.7 copy-start.4
  313.5 11.8 %copy-start.1 = (bf16[8,8,1024]{2,1,0:T(8,128)(2,1)S(1)}, bf16[8,8,1024]{2,1,0:T(8,128)(2,1)}, u32[]{:S(2)}) copy-start(bf16[8,8,1024]{2,1,0:T(8,128)(2,1)} %param.3) | copy-start | bytes 393220
Sparse Core Ops, SparseCore 0:
  9.5 76.2 all-gather.1
  217.1 96.3 reduce-scatter.1
where the time goes:
time: 338 us; the launch traced here: 333 us
  waiting for transfers between devices  153 us (45%)
  local copies, waits for them, and re-layouts  60.7 us (18%)
  matrix products  60.5 us (18%)
  other arithmetic  44.4 us (13%)
  between operations  13.9 us (4%)
    reduce_scatter x1, waiting for transfers between devices, body(): lax.psum_scatter(partial_g.astype(jnp.float32).astype(jnp.bfloat16), 'sur...  86.1 us
    all_gather x1, waiting for transfers between devices, body(): piece = lax.all_gather(up_data, 'shot', axis=1, tiled=True)  66 us
    dot_general x1, matrix products, body(): jnp.dot(piece.reshape(-1, samples), forward_table, preferred_element_type...  25.2 us
    unnamed x11, local copies, waits for them, and re-layouts  14.2 us
    dot_general x1, local copies, waits for them, and re-layouts, body(): jnp.einsum('skf,krf->rsf', down_real, up_imag, preferred_element_type=jnp...  9.99 us
    dot_general x1, local copies, waits for them, and re-layouts, body(): jnp.einsum('skf,krf->rsf', down_real, up_real, preferred_element_type=jnp...  9.94 us
    dot_general x1, local copies, waits for them, and re-layouts, body(): jnp.einsum('skf,krf->rsf', down_imag, up_real, preferred_element_type=jnp...  9.94 us
    dot_general x1, local copies, waits for them, and re-layouts, body(): jnp.einsum('skf,krf->rsf', down_imag, up_imag, preferred_element_type=jnp...  9.93 us
  transfers between devices with their start and end apart: 2, of which 2 were waited for; matrix products, arithmetic and copies ran while one was open for 6% of the time, Pallas kernels for 0%

commit v1 on v0

v1 whole, which is shorter than its diff:
```python
import functools
import math

import jax
import jax.numpy as jnp
import ml_dtypes
import numpy as np
from jax import lax
from jax.experimental import pallas as pl
from jax.experimental.pallas import tpu as pltpu
from jax.sharding import PartitionSpec as P

MESH = pl.DeviceIdType.MESH
F32 = jnp.float32
BF16 = jnp.bfloat16
LAG = 2
FG = 16


def make_tables(samples):
    freqs = samples // 2
    levels = np.arange(freqs)
    phase = (levels[:, None] * np.arange(samples)[None, :] % samples) * (2.0 * math.pi / samples)
    cosine, sine = np.cos(phase), np.sin(phase)
    norm = 1.0 / math.sqrt(samples)
    weights = np.where(levels == 0, 1.0, 2.0)[:, None]
    forward_t = np.concatenate([cosine, -sine], axis=0) * norm
    inverse = np.concatenate([weights * cosine, -weights * sine], axis=0) * norm
    return [v.astype(np.float32).astype(ml_dtypes.bfloat16) for v in (forward_t, inverse)]


def spread_matrix(shots, points):
    half = points // 2
    lane = np.arange(shots * points * FG)
    s, kk = lane // (points * FG), (lane // FG) % points
    row = (kk // half) * (shots * half) + s * half + kk % half
    return (np.arange(shots * points)[:, None] == row[None, :]).astype(ml_dtypes.bfloat16)


def line_targets(pos, j):
    out = []
    if pos >= j and pos < 3:
        out.append(pos + 1)
    if pos <= j and pos > 0:
        out.append(pos - 1)
    return out


def sends_of(w):
    v = 3 - w
    out = []
    for j in (1, 0):
        src = "own" if j == w else "big"
        for t in line_targets(w, j):
            out.append((("A", j, 0), abs(w - j), src, "z", t))
        out.append((("A", j, 0), abs(w - j), src, "y", None))
        out.append((("A", j, 0), abs(w - j), src, "c", None))
    for j in (1, 0):
        src = "own" if j == v else "transit"
        out.append((("X", j, 0), abs(v - j), src, "x", None))
        for t in line_targets(v, j):
            out.append((("T", j, 0), abs(v - j), src, "z", 3 - t))
    for j in (1, 0):
        out.append((("B", j, 0), abs(w - j) + 1, "big", "y", None))
        out.append((("B", j, 0), abs(w - j) + 1, "big", "c", None))
    for j in (1, 0):
        out.append((("A", j, 1), abs(w - j) + 1, "big", "c", None))
        out.append((("B", j, 1), abs(w - j) + 2, "big", "c", None))
    return out


def recv_slot(kind, j, yo, sib):
    return {"A": 0, "B": 1}[kind] * 8 + j * 4 + yo * 2 + sib if kind != "T" else 16 + j


def comm_kernel(up_ref, down_ref, ft_ref, spread_ref, t_ref, big, transit, down_all, e_buf, b_buf, u_buf,
                recv, send, down_recv, down_send):
    pieces = up_ref.shape[0]
    x = lax.axis_index("surf")
    b = lax.axis_index("shot")
    z, y, c = b // 4, (b // 2) % 2, b % 2
    w = jnp.where(x == 0, z, 3 - z)

    def dev(xx, ww, yy, cc):
        zz = jnp.where(xx == 0, ww, 3 - ww)
        return (zz * 4 + yy * 2 + cc, xx)

    def target(role, kind, t):
        if kind == "z":
            return dev(x, t, y, c)
        if kind == "y":
            return dev(x, role, 1 - y, c)
        if kind == "c":
            return dev(x, role, y, 1 - c)
        return dev(1 - x, 3 - role, y, c)

    barrier = pltpu.get_barrier_semaphore()
    for role in range(4):
        @pl.when(w == role)
        def _():
            peers = [("y", None), ("c", None), ("x", None)]
            peers += [("z", t) for t in (role - 1, role + 1) if 0 <= t <= 3]
            for kind, t in peers:
                pl.semaphore_signal(barrier, inc=1, device_id=target(role, kind, t), device_id_type=MESH)
            pl.semaphore_wait(barrier, len(peers))

    def slab(kind, j, yo, sib, p):
        if kind == "T":
            return transit.at[j, p]
        ab = 0 if kind == "A" else 1
        yy = y if yo == 0 else 1 - y
        cc = c if sib == 0 else 1 - c
        return big.at[ab, j, p, yy, cc]

    def copy(role, idx, p):
        (kind, j, yo), _, src, how, t = sends_of(role)[idx]
        if src == "own":
            s_ref = up_ref.at[p]
        elif src == "transit":
            s_ref = transit.at[j, p]
        else:
            s_ref = slab(kind, j, yo, 0, p)
        if kind == "T":
            d_ref, slot = transit.at[j, p], 16 + j
        elif kind == "X":
            d_ref, slot = big.at[1, j, p, y, c], recv_slot("B", j, 0, 0)
        elif how == "y":
            d_ref, slot = s_dst(kind, j, p, y, c), recv_slot(kind, j, 1, 0)
        elif how == "c":
            yy = y if yo == 0 else 1 - y
            d_ref, slot = s_dst(kind, j, p, yy, c), recv_slot(kind, j, yo, 1)
        else:
            d_ref, slot = s_dst(kind, j, p, y, c), recv_slot(kind, j, 0, 0)
        return pltpu.make_async_remote_copy(
            src_ref=s_ref, dst_ref=d_ref, send_sem=send.at[idx, p], recv_sem=recv.at[slot, p],
            device_id=target(role, how, t), device_id_type=MESH)

    def s_dst(kind, j, p, yy, cc):
        return big.at[0 if kind == "A" else 1, j, p, yy, cc]

    def arrived(kind, j, yo, sib, p):
        ref = slab(kind, j, yo, sib, p)
        pltpu.make_async_copy(ref, ref, recv.at[recv_slot(kind, j, yo, sib), p]).wait()

    down_copy = pltpu.make_async_remote_copy(
        src_ref=down_ref, dst_ref=down_all.at[1], send_sem=down_send.at[0], recv_sem=down_recv.at[0],
        device_id=(b, 1 - x), device_id_type=MESH)
    down_copy.start()

    for role in range(4):
        @pl.when(w == role)
        def _(role=role):
            sends = sends_of(role)
            streams = []
            for i, (stream, depth, src, how, t) in enumerate(sends):
                key = ("T", stream[1], 0) if stream[0] == "X" else stream
                if not streams or streams[-1][0] != key:
                    streams.append((key, depth, src, []))
                streams[-1][3].append(i)
            deepest = max(s[1] for s in streams)

            def round_(q, _):
                for key, depth, src, idxs in streams:
                    p = q - LAG * depth

                    @pl.when((p >= 0) & (p < pieces))
                    def _():
                        if src != "own":
                            arrived(*key, 0, p)
                        for i in idxs:
                            copy(role, i, p).start()
                return 0

            lax.fori_loop(0, pieces + LAG * deepest, round_, 0)
            if role <= 1:
                def keep(p, _):
                    big[0, role, p, pl.ds(y, 1), pl.ds(c, 1)] = up_ref[p][None, None]
                    return 0
                lax.fori_loop(0, pieces, keep, 0)

            def drain(p, _):
                for ab in ("A", "B"):
                    for j in (0, 1):
                        for yo in (0, 1):
                            arrived(ab, j, yo, 1, p)
                for i in range(len(sends)):
                    copy(role, i, p).wait_send()
                return 0
            lax.fori_loop(0, pieces, drain, 0)

    down_all[0] = down_ref[...]
    down_copy.wait()

    samples = ft_ref.shape[0]
    shots, half = down_ref.shape[0], down_ref.shape[1]
    groups = samples // 2 // FG
    points = 2 * half
    nt = (((1,), (1,)), ((), ()))
    flat = down_all[...].reshape(points * shots, samples)
    e_buf[...] = lax.dot_general(ft_ref[...], flat, nt, preferred_element_type=F32).astype(BF16)
    wide = points * FG
    mask = (lax.broadcasted_iota(jnp.int32, (256, shots * wide), 0) % FG
            == lax.broadcasted_iota(jnp.int32, (256, shots * wide), 1) % FG)

    def spread(i, _):
        rows = pl.ds(pl.multiple_of(i * 256, 256), 256)
        val = jnp.dot(e_buf[rows, :], spread_ref[...], preferred_element_type=F32)
        b_buf[rows, :] = jnp.where(mask, val, 0.0).astype(BF16)
        return 0
    lax.fori_loop(0, samples // 256, spread, 0)

    def forward(i, _):
        ab, kp = i // (half // 2), i % (half // 2)
        for j in (0, 1):
            rows = big[ab, j, pl.ds(2 * kp, 2)].reshape(256, samples)
            for m in range(2):
                res = lax.dot_general(ft_ref[pl.ds(512 * m, 512), :], rows, nt, preferred_element_type=F32)
                res = res.astype(BF16).reshape(groups, FG, 256)
                for n in range(2):
                    u_buf[:, m, ab * half + 2 * kp + n, :, 128 * j:128 * (j + 1)] = res[:, :, 128 * n:128 * (n + 1)]
        return 0
    lax.fori_loop(0, half, forward, 0)

    first = jnp.where(x == 0, 0, 1)

    def contract(g, _):
        re = b_buf[pl.ds(pl.multiple_of(g * FG, FG), FG), :]
        im = b_buf[pl.ds(pl.multiple_of(samples // 2 + g * FG, FG), FG), :]
        blocks = []
        for s in range(shots):
            r_s, i_s = re[:, wide * s:wide * (s + 1)], im[:, wide * s:wide * (s + 1)]
            blocks.append(jnp.concatenate([r_s, -i_s], axis=1))
            blocks.append(jnp.concatenate([i_s, r_s], axis=1))
        weights = jnp.concatenate(blocks, axis=0)
        u_g = u_buf[g].reshape(2 * wide, 256)
        res = jnp.dot(weights, u_g, preferred_element_type=F32).astype(BF16).reshape(shots, 2, FG, 256)
        t_ref[first, :, :, g] = res[..., :128]
        t_ref[1 - first, :, :, g] = res[..., 128:]
        return 0
    lax.fori_loop(0, groups, contract, 0)


def inverse_kernel(t_ref, inv_ref, len_ref, out_ref, xt):
    step = pl.program_id(1)
    shots = t_ref.shape[1]
    samples = inv_ref.shape[0]
    cols = inv_ref.shape[1]
    ramp = samples // 16

    @pl.when(step == 0)
    def _():
        parts = [t_ref[0, s].astype(F32).T for s in range(shots)]
        xt[...] = jnp.swapaxes(jnp.stack(parts, axis=0), 0, 1).astype(BF16)

    res = jnp.dot(xt[...].reshape(128 * shots, samples), inv_ref[...], preferred_element_type=F32)
    pos = (lax.broadcasted_iota(jnp.int32, (128, cols), 1) + step * cols).astype(F32)
    mute = jnp.clip((pos - len_ref[...].astype(F32) + ramp) / ramp, 0.0, 1.0)
    out_ref[...] = (res.reshape(128, shots, cols) * mute[:, None, :]).astype(BF16)


def fused_body(down_data, up_data, taper_len):
    points_half, rows, samples = up_data.shape
    shots = down_data.shape[0]
    points = 2 * points_half
    ft, inv = make_tables(samples)
    groups = samples // 2 // FG
    vmem = pl.BlockSpec(memory_space=pltpu.VMEM)
    n_send = max(len(sends_of(w)) for w in range(4))
    total = pl.pallas_call(
        comm_kernel,
        out_shape=jax.ShapeDtypeStruct((2, shots, 2, groups, FG, 128), BF16),
        in_specs=[vmem] * 4,
        out_specs=vmem,
        scratch_shapes=[
            pltpu.VMEM((2, 2, points_half, 2, 2, rows, samples), BF16),
            pltpu.VMEM((2, points_half, rows, samples), BF16),
            pltpu.VMEM((2, shots, points_half, samples), BF16),
            pltpu.VMEM((samples, shots * points), BF16),
            pltpu.VMEM((samples, shots * points * FG), BF16),
            pltpu.VMEM((groups, 2, points, FG, 256), BF16),
            pltpu.SemaphoreType.DMA((18, points_half)),
            pltpu.SemaphoreType.DMA((n_send, points_half)),
            pltpu.SemaphoreType.DMA((1,)),
            pltpu.SemaphoreType.DMA((1,)),
        ],
        compiler_params=pltpu.CompilerParams(
            collective_id=0, has_side_effects=True, vmem_limit_bytes=56 * 2**20),
        cost_estimate=pl.CostEstimate(flops=12 * 10**9, bytes_accessed=2**24, transcendentals=0),
    )(up_data, down_data, jnp.asarray(ft), jnp.asarray(spread_matrix(shots, points)))
    total = total.reshape(2, shots, samples, 128)
    cols = 256
    return pl.pallas_call(
        inverse_kernel,
        out_shape=jax.ShapeDtypeStruct((256, shots, samples), BF16),
        grid=(2, samples // cols),
        in_specs=[
            pl.BlockSpec((1, shots, samples, 128), lambda i, t: (i, 0, 0, 0)),
            pl.BlockSpec((samples, cols), lambda i, t: (0, t)),
            pl.BlockSpec((128, 1), lambda i, t: (i, 0)),
        ],
        out_specs=pl.BlockSpec((128, shots, cols), lambda i, t: (i, 0, t)),
        scratch_shapes=[pltpu.VMEM((128, shots, samples), BF16)],
        compiler_params=pltpu.CompilerParams(vmem_limit_bytes=48 * 2**20),
        cost_estimate=pl.CostEstimate(flops=43 * 10**8, bytes_accessed=2**23, transcendentals=0),
    )(total, jnp.asarray(inv), taper_len[:, None])


def plain_body(down_data, up_data, taper_len):
    shots, points, samples = down_data.shape
    freqs = samples // 2
    ft, inv = make_tables(samples)
    forward_table, inverse_table = jnp.asarray(ft).T, jnp.asarray(inv)

    def spectra(data):
        flat = jnp.dot(data.reshape(-1, samples), forward_table, preferred_element_type=F32)
        flat = flat.astype(BF16).reshape(data.shape)
        return flat[:, :, :freqs], flat[:, :, freqs:]

    mul = functools.partial(jnp.einsum, "skf,krf->rsf", preferred_element_type=F32)
    dr, di = spectra(down_data)
    ur, ui = (lax.all_gather(u, "shot", axis=1, tiled=True) for u in spectra(up_data))
    partial = jnp.concatenate([mul(dr, ur) - mul(di, ui), mul(dr, ui) + mul(di, ur)], axis=2)
    total = lax.psum_scatter(partial.astype(BF16), "surf", scatter_dimension=0, tiled=True)
    trace = jnp.einsum("rsf,ft->rst", total, inverse_table, preferred_element_type=F32)
    ramp = samples // 16
    pos = jnp.arange(samples, dtype=F32)
    mute = jnp.clip((pos[None, :] - taper_len.astype(F32)[:, None] + ramp) / ramp, 0.0, 1.0)
    return (trace * mute[:, None, :]).astype(BF16)


def solution(mesh):
    placed = (P("shot", "surf", None), P("surf", "shot", None), P("surf"))
    fits = mesh.shape["shot"] == 16 and mesh.shape["surf"] == 2
    return jax.shard_map(
        fused_body if fits else plain_body,
        mesh=mesh, in_specs=placed, out_specs=P("surf", "shot", None), check_vma=False)
```

time: 338 us -> 101 us (0.30); the launches traced: 333 us -> 100 us
  waiting for transfers between devices: 153 us -> 0 us
  Pallas kernels: 0 us -> 99.1 us
  matrix products: 60.5 us -> 0 us
  local copies, waits for them, and re-layouts: 60.7 us -> 0.81 us
  other arithmetic: 44.4 us -> 0 us
  between operations: 13.9 us -> 0.03 us
    pallas_call x0 -> x2, Pallas kernels: none -> 99.1 us  [the longest x1 86.7 us: fused_body(): pl.pallas_call(comm_kernel, out_shape=jax.ShapeDtypeStruct((2, shots, 2,...]
    reduce_scatter x1 -> x0, waiting for transfers between devices: 86.1 us -> none  [body(): lax.psum_scatter(partial_g.astype(jnp.float32).astype(jnp.bfloat16), 'sur...]
    all_gather x1 -> x0, waiting for transfers between devices: 66 us -> none  [body(): piece = lax.all_gather(up_data, 'shot', axis=1, tiled=True)]
    dot_general x7 -> x0, matrix products: 60.5 us -> none  [the longest x1 25.2 us: body(): jnp.dot(piece.reshape(-1, samples), forward_table, preferred_element_type...]
    dot_general x4 -> x0, local copies, waits for them, and re-layouts: 39.8 us -> none  [the longest x1 9.99 us: body(): jnp.einsum('skf,krf->rsf', down_real, up_imag, preferred_element_type=jnp...]
    unnamed x11 -> x2, local copies, waits for them, and re-layouts: 14.2 us -> 0.01 us
    mul x1 -> x0, other arithmetic: 9.46 us -> none  [make_tables(): -weights * sine]
    sub x1 -> x0, other arithmetic: 9.44 us -> none  [body(): jnp.einsum('skf,krf->rsf', down_real, up_real, preferred_element_type=jnp...]
  transfers between devices with their start and end apart: 2 -> 0, of which waited for: 2 -> 0; matrix products, arithmetic and copies ran while one was open for 6% -> 0% of each run, Pallas kernels for 0% -> 0%
where the time goes in v1:
time: 101 us; the launch traced here: 100 us
  Pallas kernels  99.1 us (98%)
    pallas_call x1, Pallas kernels, fused_body(): pl.pallas_call(comm_kernel, out_shape=jax.ShapeDtypeStruct((2, shots, 2,...  86.7 us
    pallas_call x1, Pallas kernels, fused_body(): pl.pallas_call(inverse_kernel, out_shape=jax.ShapeDtypeStruct((256, shots...  12.5 us

profile of v1, /device:TPU:2, one launch (start us, length us, event | category | flops | bytes accessed | tf_op | source)
XLA Modules:
  0.0 100.0 jit_solution(2867278309480361202)
XLA Ops:
  0.0 0.8 copy.7.len_ref
  0.8 0.0 copy-start
  0.8 86.7 %shard_map.64 = bf16[2,8,2,32,16,128]{5,4,3,2,1,0:T(8,128)(2,1)} custom-call(bf16[8,32,1024]{2,1,0:T(8,128)(2,1)} %up_ref.1, bf16[8,8,1024]{2,1,0:T(8,128)(2,1)} %down_ref.1, bf16[1024,1024]{1,0:T(8,128)(2,1)} %constant.6.clone.ft_ref, bf16[128,2048]{1,0:T(8,128)(2,1)} %constant.7.clone.spread_ref), custom_call_target="tpu_custom_call" | custom-call | flops 12000000000 | bytes 16777216 | tf_op jit(solution)/shard_map/pallas_call | solution.py:269
  87.5 0.0 copy-done
  87.5 12.5 %shard_map.65 = bf16[256,8,1024]{2,1,0:T(8,128)(2,1)} custom-call(bf16[2,8,1024,128]{3,2,1,0:T(8,128)(2,1)} %bitcast.3, bf16[1024,1024]{1,0:T(8,128)(2,1)S(1)} %copy-done, s32[256,1]{1,0:T(8,128)S(1)} %copy.7.len_ref), custom_call_target="tpu_custom_call" | custom-call | flops 4300000256 | bytes 8388608 | tf_op jit(solution)/shard_map/pallas_call | solution.py:292
Async XLA Ops:
  0.8 86.7 %copy-start = (bf16[1024,1024]{1,0:T(8,128)(2,1)S(1)}, bf16[1024,1024]{1,0:T(8,128)(2,1)}, u32[]{:S(2)}) copy-start(bf16[1024,1024]{1,0:T(8,128)(2,1)} %constant.8.clone.inv_ref) | copy-start | bytes 6291460

commit v2 on v1

--- a/solution.py
+++ b/solution.py
@@ -13,7 +13,9 @@
 MESH = pl.DeviceIdType.MESH
 F32 = jnp.float32
 BF16 = jnp.bfloat16
-LAG = 2
+LAG = 1
+SPREAD_AT = 3
+ROWS = 64
 FG = 16
 
 
@@ -73,7 +75,7 @@
     return {"A": 0, "B": 1}[kind] * 8 + j * 4 + yo * 2 + sib if kind != "T" else 16 + j
 
 
-def comm_kernel(up_ref, down_ref, ft_ref, spread_ref, t_ref, big, transit, down_all, e_buf, b_buf, u_buf,
+def comm_kernel(up_ref, down_ref, ft_ref, spread_ref, t_ref, big, transit, down_all, e_buf, b_buf, u_buf, xf,
                 recv, send, down_recv, down_send):
     pieces = up_ref.shape[0]
     x = lax.axis_index("surf")
@@ -147,115 +149,136 @@
         device_id=(b, 1 - x), device_id_type=MESH)
     down_copy.start()
 
-    for role in range(4):
-        @pl.when(w == role)
-        def _(role=role):
-            sends = sends_of(role)
-            streams = []
-            for i, (stream, depth, src, how, t) in enumerate(sends):
-                key = ("T", stream[1], 0) if stream[0] == "X" else stream
-                if not streams or streams[-1][0] != key:
-                    streams.append((key, depth, src, []))
-                streams[-1][3].append(i)
-            deepest = max(s[1] for s in streams)
-
-            def round_(q, _):
-                for key, depth, src, idxs in streams:
-                    p = q - LAG * depth
-
-                    @pl.when((p >= 0) & (p < pieces))
-                    def _():
-                        if src != "own":
-                            arrived(*key, 0, p)
-                        for i in idxs:
-                            copy(role, i, p).start()
-                return 0
-
-            lax.fori_loop(0, pieces + LAG * deepest, round_, 0)
-            if role <= 1:
-                def keep(p, _):
-                    big[0, role, p, pl.ds(y, 1), pl.ds(c, 1)] = up_ref[p][None, None]
-                    return 0
-                lax.fori_loop(0, pieces, keep, 0)
-
-            def drain(p, _):
-                for ab in ("A", "B"):
-                    for j in (0, 1):
-                        for yo in (0, 1):
-                            arrived(ab, j, yo, 1, p)
-                for i in range(len(sends)):
-                    copy(role, i, p).wait_send()
-                return 0
-            lax.fori_loop(0, pieces, drain, 0)
-
-    down_all[0] = down_ref[...]
-    down_copy.wait()
-
     samples = ft_ref.shape[0]
     shots, half = down_ref.shape[0], down_ref.shape[1]
     groups = samples // 2 // FG
     points = 2 * half
+    wide = points * FG
     nt = (((1,), (1,)), ((), ()))
-    flat = down_all[...].reshape(points * shots, samples)
-    e_buf[...] = lax.dot_general(ft_ref[...], flat, nt, preferred_element_type=F32).astype(BF16)
-    wide = points * FG
-    mask = (lax.broadcasted_iota(jnp.int32, (256, shots * wide), 0) % FG
-            == lax.broadcasted_iota(jnp.int32, (256, shots * wide), 1) % FG)
-
-    def spread(i, _):
-        rows = pl.ds(pl.multiple_of(i * 256, 256), 256)
-        val = jnp.dot(e_buf[rows, :], spread_ref[...], preferred_element_type=F32)
-        b_buf[rows, :] = jnp.where(mask, val, 0.0).astype(BF16)
-        return 0
-    lax.fori_loop(0, samples // 256, spread, 0)
-
-    def forward(i, _):
-        ab, kp = i // (half // 2), i % (half // 2)
-        for j in (0, 1):
-            rows = big[ab, j, pl.ds(2 * kp, 2)].reshape(256, samples)
+
+    for role in range(2):
+        @pl.when(w == role)
+        def _(role=role):
+            def keep(p, _):
+                big[0, role, p, pl.ds(y, 1), pl.ds(c, 1)] = up_ref[p][None, None]
+                return 0
+            lax.fori_loop(0, pieces, keep, 0)
+
+    def relay(role, q):
+        streams = []
+        for i, (stream, depth, src, how, t) in enumerate(sends_of(role)):
+            key = ("T", stream[1], 0) if stream[0] == "X" else stream
+            if not streams or streams[-1][0] != key:
+                streams.append((key, depth, src, []))
+            streams[-1][3].append(i)
+        for key, depth, src, idxs in streams:
+            p = q - LAG * depth
+
+            @pl.when((p >= 0) & (p < pieces))
+            def _():
+                if src != "own":
+                    arrived(*key, 0, p)
+                for i in idxs:
+                    copy(role, i, p).start()
+
+    def spread():
+        down_all[0] = down_ref[...]
+        down_copy.wait()
+        flat = down_all[...].reshape(points * shots, samples)
+        e_buf[...] = lax.dot_general(ft_ref[...], flat, nt, preferred_element_type=F32).astype(BF16)
+        mask = (lax.broadcasted_iota(jnp.int32, (256, shots * wide), 0) % FG
+                == lax.broadcasted_iota(jnp.int32, (256, shots * wide), 1) % FG)
+
+        def chunk(i, _):
+            rows = pl.ds(pl.multiple_of(i * 256, 256), 256)
+            val = jnp.dot(e_buf[rows, :], spread_ref[...], preferred_element_type=F32)
+            b_buf[rows, :] = jnp.where(mask, val, 0.0).astype(BF16)
+            return 0
+        lax.fori_loop(0, samples // 256, chunk, 0)
+
+    def forward(p):
+        for ab in (0, 1):
+            rows = big[ab, :, pl.ds(p, 1)].reshape(256, samples)
             for m in range(2):
                 res = lax.dot_general(ft_ref[pl.ds(512 * m, 512), :], rows, nt, preferred_element_type=F32)
-                res = res.astype(BF16).reshape(groups, FG, 256)
-                for n in range(2):
-                    u_buf[:, m, ab * half + 2 * kp + n, :, 128 * j:128 * (j + 1)] = res[:, :, 128 * n:128 * (n + 1)]
+                u_buf[:, m, ab * half + p] = res.astype(BF16).reshape(groups, FG, 256)
+
+    late = LAG * 5 + 1
+
+    def round_(q, _):
+        for role in range(4):
+            @pl.when(w == role)
+            def _(role=role):
+                relay(role, q)
+
+        @pl.when(q == SPREAD_AT)
+        def _():
+            spread()
+
+        p = q - late
+
+        @pl.when(p >= 0)
+        def _():
+            for ab in ("A", "B"):
+                for j in (0, 1):
+                    for yo in (0, 1):
+                        arrived(ab, j, yo, 1, p)
+            forward(p)
         return 0
-    lax.fori_loop(0, half, forward, 0)
+
+    lax.fori_loop(0, pieces + late, round_, 0)
 
     first = jnp.where(x == 0, 0, 1)
-
-    def contract(g, _):
-        re = b_buf[pl.ds(pl.multiple_of(g * FG, FG), FG), :]
-        im = b_buf[pl.ds(pl.multiple_of(samples // 2 + g * FG, FG), FG), :]
-        blocks = []
+    per = 128 // FG
+
+    def contract(gb, _):
+        res = []
+        for gi in range(per):
+            g = gb * per + gi
+            re = b_buf[pl.ds(pl.multiple_of(g * FG, FG), FG), :]
+            im = b_buf[pl.ds(pl.multiple_of(samples // 2 + g * FG, FG), FG), :]
+            blocks = []
+            for s in range(shots):
+                r_s, i_s = re[:, wide * s:wide * (s + 1)], im[:, wide * s:wide * (s + 1)]
+                blocks.append(jnp.concatenate([r_s, -i_s], axis=1))
+                blocks.append(jnp.concatenate([i_s, r_s], axis=1))
+            weights = jnp.concatenate(blocks, axis=0)
+            res.append(jnp.dot(weights, u_buf[g].reshape(2 * wide, 256), preferred_element_type=F32))
         for s in range(shots):
-            r_s, i_s = re[:, wide * s:wide * (s + 1)], im[:, wide * s:wide * (s + 1)]
-            blocks.append(jnp.concatenate([r_s, -i_s], axis=1))
-            blocks.append(jnp.concatenate([i_s, r_s], axis=1))
-        weights = jnp.concatenate(blocks, axis=0)
-        u_g = u_buf[g].reshape(2 * wide, 256)
-        res = jnp.dot(weights, u_g, preferred_element_type=F32).astype(BF16).reshape(shots, 2, FG, 256)
-        t_ref[first, :, :, g] = res[..., :128]
-        t_ref[1 - first, :, :, g] = res[..., 128:]
+            for cc in range(2):
+                at = (s * 2 + cc) * FG
+                val = jnp.concatenate([r[at:at + FG] for r in res], axis=0)
+                xf[cc, pl.ds(s, 256, stride=shots), :] = val.T
+        for cc in range(2):
+            lanes = pl.ds(pl.multiple_of(cc * (samples // 2) + gb * 128, 128), 128)
+            for j in range(2):
+                h = first if j == 0 else 1 - first
+                t_ref[pl.ds(pl.multiple_of(h * 128 * shots, 128), 128 * shots), lanes] = (
+                    xf[cc, pl.ds(128 * shots * j, 128 * shots), :].astype(BF16))
         return 0
-    lax.fori_loop(0, groups, contract, 0)
-
-
-def inverse_kernel(t_ref, inv_ref, len_ref, out_ref, xt):
-    step = pl.program_id(1)
-    shots = t_ref.shape[1]
-    samples = inv_ref.shape[0]
-    cols = inv_ref.shape[1]
+    lax.fori_loop(0, groups // per, contract, 0)
+
+    for role in range(4):
+        @pl.when(w == role)
+        def _(role=role):
+            def drain(p, _):
+                for i in range(len(sends_of(role))):
+                    copy(role, i, p).wait_send()
+                return 0
+            lax.fori_loop(0, pieces, drain, 0)
+
+
+def inverse_kernel(t_ref, inv_ref, len_ref, out_ref):
+    rows, shots, samples = out_ref.shape
     ramp = samples // 16
-
-    @pl.when(step == 0)
-    def _():
-        parts = [t_ref[0, s].astype(F32).T for s in range(shots)]
-        xt[...] = jnp.swapaxes(jnp.stack(parts, axis=0), 0, 1).astype(BF16)
-
-    res = jnp.dot(xt[...].reshape(128 * shots, samples), inv_ref[...], preferred_element_type=F32)
-    pos = (lax.broadcasted_iota(jnp.int32, (128, cols), 1) + step * cols).astype(F32)
-    mute = jnp.clip((pos - len_ref[...].astype(F32) + ramp) / ramp, 0.0, 1.0)
-    out_ref[...] = (res.reshape(128, shots, cols) * mute[:, None, :]).astype(BF16)
+    lens = jnp.broadcast_to(len_ref[...].astype(F32), (rows, len_ref.shape[1]))
+    own = (lax.broadcasted_iota(jnp.int32, lens.shape, 1)
+           == lax.broadcasted_iota(jnp.int32, lens.shape, 0) + pl.program_id(0) * rows)
+    column = jnp.sum(jnp.where(own, lens, 0.0), axis=1, keepdims=True)
+    res = jnp.dot(t_ref[...], inv_ref[...], preferred_element_type=F32)
+    pos = lax.broadcasted_iota(jnp.int32, (rows, samples), 1).astype(F32)
+    mute = jnp.clip((pos - column + ramp) / ramp, 0.0, 1.0)
+    out_ref[...] = (res.reshape(rows, shots, samples) * mute[:, None, :]).astype(BF16)
 
 
 def fused_body(down_data, up_data, taper_len):
@@ -268,7 +291,7 @@
     n_send = max(len(sends_of(w)) for w in range(4))
     total = pl.pallas_call(
         comm_kernel,
-        out_shape=jax.ShapeDtypeStruct((2, shots, 2, groups, FG, 128), BF16),
+        out_shape=jax.ShapeDtypeStruct((256 * shots, samples), BF16),
         in_specs=[vmem] * 4,
         out_specs=vmem,
         scratch_shapes=[
@@ -278,6 +301,7 @@
             pltpu.VMEM((samples, shots * points), BF16),
             pltpu.VMEM((samples, shots * points * FG), BF16),
             pltpu.VMEM((groups, 2, points, FG, 256), BF16),
+            pltpu.VMEM((2, 256 * shots, 128), F32),
             pltpu.SemaphoreType.DMA((18, points_half)),
             pltpu.SemaphoreType.DMA((n_send, points_half)),
             pltpu.SemaphoreType.DMA((1,)),
@@ -287,22 +311,19 @@
             collective_id=0, has_side_effects=True, vmem_limit_bytes=56 * 2**20),
         cost_estimate=pl.CostEstimate(flops=12 * 10**9, bytes_accessed=2**24, transcendentals=0),
     )(up_data, down_data, jnp.asarray(ft), jnp.asarray(spread_matrix(shots, points)))
-    total = total.reshape(2, shots, samples, 128)
-    cols = 256
     return pl.pallas_call(
         inverse_kernel,
         out_shape=jax.ShapeDtypeStruct((256, shots, samples), BF16),
-        grid=(2, samples // cols),
+        grid=(256 // ROWS,),
         in_specs=[
-            pl.BlockSpec((1, shots, samples, 128), lambda i, t: (i, 0, 0, 0)),
-            pl.BlockSpec((samples, cols), lambda i, t: (0, t)),
-            pl.BlockSpec((128, 1), lambda i, t: (i, 0)),
+            pl.BlockSpec((ROWS * shots, samples), lambda i: (i, 0)),
+            pl.BlockSpec((samples, samples), lambda i: (0, 0)),
+            pl.BlockSpec((1, 256), lambda i: (0, 0)),
         ],
-        out_specs=pl.BlockSpec((128, shots, cols), lambda i, t: (i, 0, t)),
-        scratch_shapes=[pltpu.VMEM((128, shots, samples), BF16)],
+        out_specs=pl.BlockSpec((ROWS, shots, samples), lambda i: (i, 0, 0)),
         compiler_params=pltpu.CompilerParams(vmem_limit_bytes=48 * 2**20),
         cost_estimate=pl.CostEstimate(flops=43 * 10**8, bytes_accessed=2**23, transcendentals=0),
-    )(total, jnp.asarray(inv), taper_len[:, None])
+    )(total, jnp.asarray(inv), taper_len[None, :])
 
 
 def plain_body(down_data, up_data, taper_len):

time: 101 us -> 82.9 us (0.82)
  Pallas kernels: 99.1 us -> 82.3 us
    pallas_call x1, Pallas kernels: 86.7 us -> 74.5 us  [fused_body(): pl.pallas_call(comm_kernel, out_shape=jax.ShapeDtypeStruct((256 * shots,...]
    pallas_call x1, Pallas kernels: 12.5 us -> 7.78 us  [fused_body(): pl.pallas_call(inverse_kernel, out_shape=jax.ShapeDtypeStruct((256, shots...]
where the time goes in v2:
time: 82.9 us; the launch traced here: 82.3 us
  Pallas kernels  82.3 us (99%)
    pallas_call x1, Pallas kernels, fused_body(): pl.pallas_call(comm_kernel, out_shape=jax.ShapeDtypeStruct((256 * shots,...  74.5 us
    pallas_call x1, Pallas kernels, fused_body(): pl.pallas_call(inverse_kernel, out_shape=jax.ShapeDtypeStruct((256, shots...  7.78 us

profile of v2, /device:TPU:2, one launch (start us, length us, event | category | flops | bytes accessed | tf_op | source)
XLA Modules:
  0.0 82.3 jit_solution(2513104912691266192)
XLA Ops:
  0.0 0.0 copy-start
  0.0 0.0 copy-start.1
  0.0 74.5 %shard_map.64.t_ref = bf16[2048,1024]{1,0:T(8,128)(2,1)} custom-call(bf16[8,32,1024]{2,1,0:T(8,128)(2,1)} %up_ref.1, bf16[8,8,1024]{2,1,0:T(8,128)(2,1)} %down_ref.1, bf16[1024,1024]{1,0:T(8,128)(2,1)} %constant.6.clone.ft_ref, bf16[128,2048]{1,0:T(8,128)(2,1)} %constant.7.clone.spread_ref), custom_call_target="tpu_custom_call" | custom-call | flops 12000000000 | bytes 16777216 | tf_op jit(solution)/shard_map/pallas_call | solution.py:292
  74.5 0.0 copy-done
  74.5 0.0 copy-done.1
  74.5 7.8 %shard_map.65 = bf16[256,8,1024]{2,1,0:T(8,128)(2,1)} custom-call(bf16[2048,1024]{1,0:T(8,128)(2,1)} %shard_map.64.t_ref, bf16[1024,1024]{1,0:T(8,128)(2,1)S(1)} %copy-done.1, s32[1,256]{1,0:T(1,128)S(1)} %bitcast.1), custom_call_target="tpu_custom_call" | custom-call | flops 4300000256 | bytes 8388608 | tf_op jit(solution)/shard_map/pallas_call | solution.py:314
Async XLA Ops:
  0.0 74.5 %copy-start = (s32[256]{0:T(256)S(1)}, s32[256]{0:T(256)}, u32[]{:S(2)}) copy-start(s32[256]{0:T(256)} %param.8) | copy-start | bytes 3076
  0.0 74.5 %copy-start.1 = (bf16[1024,1024]{1,0:T(8,128)(2,1)S(1)}, bf16[1024,1024]{1,0:T(8,128)(2,1)}, u32[]{:S(2)}) copy-start(bf16[1024,1024]{1,0:T(8,128)(2,1)} %constant.8.clone.inv_ref) | copy-start | bytes 6291460

commit v3 on v2

--- a/solution.py
+++ b/solution.py
@@ -46,6 +46,14 @@
     if pos <= j and pos > 0:
         out.append(pos - 1)
     return out
+
+
+VIA_Z = ((0, 2), (1, 0), (2, 2), (4, 4))
+
+
+def along_z(pos, j, p):
+    n = VIA_Z[pos][j]
+    return (p % n == n - 1) if n else False
 
 
 def sends_of(w):
@@ -66,9 +74,28 @@
         out.append((("B", j, 0), abs(w - j) + 1, "big", "y", None))
         out.append((("B", j, 0), abs(w - j) + 1, "big", "c", None))
     for j in (1, 0):
+        for t in line_targets(w, j):
+            if VIA_Z[t][j]:
+                out.append((("A", j, 1), abs(w - j) + 1, "big", "z", t))
         out.append((("A", j, 1), abs(w - j) + 1, "big", "c", None))
         out.append((("B", j, 1), abs(w - j) + 2, "big", "c", None))
     return out
+
+
+def guard(w, send, p):
+    (kind, j, yo), _, _, how, t = send
+    if kind == "A" and yo == 1 and how == "z":
+        return None if VIA_Z[t][j] == 1 else along_z(t, j, p)
+    if kind == "A" and yo == 0 and how == "y" and VIA_Z[w][j]:
+        return False if VIA_Z[w][j] == 1 else jnp.logical_not(along_z(w, j, p))
+    return None
+
+
+def when(cond, f):
+    if cond is None:
+        f()
+    elif cond is not False:
+        pl.when(cond)(f)
 
 
 def recv_slot(kind, j, yo, sib):
@@ -122,6 +149,7 @@
             s_ref = transit.at[j, p]
         else:
             s_ref = slab(kind, j, yo, 0, p)
+        yy = y if yo == 0 else 1 - y
         if kind == "T":
             d_ref, slot = transit.at[j, p], 16 + j
         elif kind == "X":
@@ -129,10 +157,9 @@
         elif how == "y":
             d_ref, slot = s_dst(kind, j, p, y, c), recv_slot(kind, j, 1, 0)
         elif how == "c":
-            yy = y if yo == 0 else 1 - y
             d_ref, slot = s_dst(kind, j, p, yy, c), recv_slot(kind, j, yo, 1)
         else:
-            d_ref, slot = s_dst(kind, j, p, y, c), recv_slot(kind, j, 0, 0)
+            d_ref, slot = s_dst(kind, j, p, yy, c), recv_slot(kind, j, yo, 0)
         return pltpu.make_async_remote_copy(
             src_ref=s_ref, dst_ref=d_ref, send_sem=send.at[idx, p], recv_sem=recv.at[slot, p],
             device_id=target(role, how, t), device_id_type=MESH)
@@ -163,6 +190,12 @@
                 big[0, role, p, pl.ds(y, 1), pl.ds(c, 1)] = up_ref[p][None, None]
                 return 0
             lax.fori_loop(0, pieces, keep, 0)
+
+    def start(role, i, p):
+        copy(role, i, p).start()
+
+    def sent(role, i, p):
+        copy(role, i, p).wait_send()
 
     def relay(role, q):
         streams = []
@@ -179,7 +212,7 @@
                 if src != "own":
                     arrived(*key, 0, p)
                 for i in idxs:
-                    copy(role, i, p).start()
+                    when(guard(role, sends_of(role)[i], p), functools.partial(start, role, i, p))
 
     def spread():
         down_all[0] = down_ref[...]
@@ -262,8 +295,8 @@
         @pl.when(w == role)
         def _(role=role):
             def drain(p, _):
-                for i in range(len(sends_of(role))):
-                    copy(role, i, p).wait_send()
+                for i, one in enumerate(sends_of(role)):
+                    when(guard(role, one, p), functools.partial(sent, role, i, p))
                 return 0
             lax.fori_loop(0, pieces, drain, 0)
 

time: 82.9 us -> 78.4 us (0.946)
  Pallas kernels: 82.3 us -> 78.2 us
    pallas_call x1, Pallas kernels: 74.5 us -> 70.4 us  [fused_body(): pl.pallas_call(comm_kernel, out_shape=jax.ShapeDtypeStruct((256 * shots,...]
where the time goes in v3:
time: 78.4 us; the launch traced here: 78.2 us
  Pallas kernels  78.2 us (100%)
    pallas_call x1, Pallas kernels, fused_body(): pl.pallas_call(comm_kernel, out_shape=jax.ShapeDtypeStruct((256 * shots,...  70.4 us
    pallas_call x1, Pallas kernels, fused_body(): pl.pallas_call(inverse_kernel, out_shape=jax.ShapeDtypeStruct((256, shots...  7.77 us

profile of v3, /device:TPU:2, one launch (start us, length us, event | category | flops | bytes accessed | tf_op | source)
XLA Modules:
  0.0 78.2 jit_solution(1426690384774340345)
XLA Ops:
  0.0 0.0 copy-start
  0.0 0.0 copy-start.1
  0.0 70.4 %shard_map.64.t_ref = bf16[2048,1024]{1,0:T(8,128)(2,1)} custom-call(bf16[8,32,1024]{2,1,0:T(8,128)(2,1)} %up_ref.1, bf16[8,8,1024]{2,1,0:T(8,128)(2,1)} %down_ref.1, bf16[1024,1024]{1,0:T(8,128)(2,1)} %constant.6.clone.ft_ref, bf16[128,2048]{1,0:T(8,128)(2,1)} %constant.7.clone.spread_ref), custom_call_target="tpu_custom_call" | custom-call | flops 12000000000 | bytes 16777216 | tf_op jit(solution)/shard_map/pallas_call | solution.py:325
  70.4 0.0 copy-done
  70.4 0.0 copy-done.1
  70.4 7.8 %shard_map.65 = bf16[256,8,1024]{2,1,0:T(8,128)(2,1)} custom-call(bf16[2048,1024]{1,0:T(8,128)(2,1)} %shard_map.64.t_ref, bf16[1024,1024]{1,0:T(8,128)(2,1)S(1)} %copy-done.1, s32[1,256]{1,0:T(1,128)S(1)} %bitcast.1), custom_call_target="tpu_custom_call" | custom-call | flops 4300000256 | bytes 8388608 | tf_op jit(solution)/shard_map/pallas_call | solution.py:347
Async XLA Ops:
  0.0 70.4 %copy-start = (s32[256]{0:T(256)S(1)}, s32[256]{0:T(256)}, u32[]{:S(2)}) copy-start(s32[256]{0:T(256)} %param.8) | copy-start | bytes 3076
  0.0 70.4 %copy-start.1 = (bf16[1024,1024]{1,0:T(8,128)(2,1)S(1)}, bf16[1024,1024]{1,0:T(8,128)(2,1)}, u32[]{:S(2)}) copy-start(bf16[1024,1024]{1,0:T(8,128)(2,1)} %constant.8.clone.inv_ref) | copy-start | bytes 6291460

commit v4 on v3

--- a/solution.py
+++ b/solution.py
@@ -60,16 +60,16 @@
     v = 3 - w
     out = []
     for j in (1, 0):
+        src = "own" if j == v else "transit"
+        out.append((("X", j, 0), abs(v - j), src, "x", None))
+        for t in line_targets(v, j):
+            out.append((("T", j, 0), abs(v - j), src, "z", 3 - t))
+    for j in (1, 0):
         src = "own" if j == w else "big"
         for t in line_targets(w, j):
             out.append((("A", j, 0), abs(w - j), src, "z", t))
         out.append((("A", j, 0), abs(w - j), src, "y", None))
         out.append((("A", j, 0), abs(w - j), src, "c", None))
-    for j in (1, 0):
-        src = "own" if j == v else "transit"
-        out.append((("X", j, 0), abs(v - j), src, "x", None))
-        for t in line_targets(v, j):
-            out.append((("T", j, 0), abs(v - j), src, "z", 3 - t))
     for j in (1, 0):
         out.append((("B", j, 0), abs(w - j) + 1, "big", "y", None))
         out.append((("B", j, 0), abs(w - j) + 1, "big", "c", None))

time: 78.4 us -> 78.9 us (level)
  no operation moved by 1% of the time
where the time goes in v4:
time: 78.9 us; the launch traced here: 78.6 us
  Pallas kernels  78.6 us (100%)
    pallas_call x1, Pallas kernels, fused_body(): pl.pallas_call(comm_kernel, out_shape=jax.ShapeDtypeStruct((256 * shots,...  70.8 us
    pallas_call x1, Pallas kernels, fused_body(): pl.pallas_call(inverse_kernel, out_shape=jax.ShapeDtypeStruct((256, shots...  7.77 us

profile of v4, /device:TPU:2, one launch (start us, length us, event | category | flops | bytes accessed | tf_op | source)
XLA Modules:
  0.0 78.6 jit_solution(1667676401494418141)
XLA Ops:
  0.0 0.0 copy-start
  0.0 0.0 copy-start.1
  0.0 70.8 %shard_map.64.t_ref = bf16[2048,1024]{1,0:T(8,128)(2,1)} custom-call(bf16[8,32,1024]{2,1,0:T(8,128)(2,1)} %up_ref.1, bf16[8,8,1024]{2,1,0:T(8,128)(2,1)} %down_ref.1, bf16[1024,1024]{1,0:T(8,128)(2,1)} %constant.6.clone.ft_ref, bf16[128,2048]{1,0:T(8,128)(2,1)} %constant.7.clone.spread_ref), custom_call_target="tpu_custom_call" | custom-call | flops 12000000000 | bytes 16777216 | tf_op jit(solution)/shard_map/pallas_call | solution.py:325
  70.9 0.0 copy-done
  70.9 0.0 copy-done.1
  70.9 7.8 %shard_map.65 = bf16[256,8,1024]{2,1,0:T(8,128)(2,1)} custom-call(bf16[2048,1024]{1,0:T(8,128)(2,1)} %shard_map.64.t_ref, bf16[1024,1024]{1,0:T(8,128)(2,1)S(1)} %copy-done.1, s32[1,256]{1,0:T(1,128)S(1)} %bitcast.1), custom_call_target="tpu_custom_call" | custom-call | flops 4300000256 | bytes 8388608 | tf_op jit(solution)/shard_map/pallas_call | solution.py:347
Async XLA Ops:
  0.0 70.9 %copy-start = (s32[256]{0:T(256)S(1)}, s32[256]{0:T(256)}, u32[]{:S(2)}) copy-start(s32[256]{0:T(256)} %param.8) | copy-start | bytes 3076
  0.0 70.9 %copy-start.1 = (bf16[1024,1024]{1,0:T(8,128)(2,1)S(1)}, bf16[1024,1024]{1,0:T(8,128)(2,1)}, u32[]{:S(2)}) copy-start(bf16[1024,1024]{1,0:T(8,128)(2,1)} %constant.8.clone.inv_ref) | copy-start | bytes 6291460
